TPU v7x, 32 devices: a whole 2x2x4 slice. The times are simulated.
32 devices in a mesh: dp: 8 (over y, x, core), expert: 4 (over z).
Axes of the slice: x: 2, y: 2, z: 4, core: 2. Of those that a mesh axis runs over, the one named last changes fastest.
Arguments:
- grad_rows: bfloat16 [4096, 3584], P(('dp', 'expert')), may hold values from -6 to 6
- grad_exponent: int32 [4096, 28], P(('dp', 'expert')), may hold values from 0 to 3
- gate: bfloat16 [4096], P(('dp', 'expert')), may hold values from 0.049804688 to 1
- routing: int32 [4096, 1], P(('dp', 'expert')), may hold values from 0 to 3; in each aligned block of 128 rows (0 to 127, 128 to 255, ...) at most 34 rows name the same one
- saved_hidden: bfloat16 [8, 4, 136, 1024], P('dp', 'expert'), may hold values from -6 to 6
- down_weight: bfloat16 [4, 1024, 3584], P('expert'), may hold values from -0.1875 to 0.1875
Outputs:
- hidden_grad: bfloat16 [8, 4, 136, 1024], P('dp', 'expert')
- weight_grad: float32 [4, 1024, 3584], P('expert', 'dp')
- gate_grad: float32 [4096], P(('dp', 'expert'))
Inputs may be any that keep to these rules, and one draw needn't show every extreme that they name: `routing`: within one device's 128 rows no expert is named more than 34 times; in some device's rows one expert is named exactly 34 times.
All inputs are finite; a program needn't handle non-finite values.
Results may differ from a plain program's by a relative error of at most 0.0095.
Values may be sent and summed in bfloat16 or wider, within the bound.
A program may use at most 64 MiB of HBM per device.

v0:
```python
import jax
import jax.numpy as jnp
from jax import lax
from jax.sharding import PartitionSpec as P


def slot_table(route, experts, cap):
    onehot = (route[:, None] == jnp.arange(experts, dtype=jnp.int32)[None, :]).astype(jnp.int32)
    before = jnp.cumsum(onehot, axis=0) - onehot
    rank = jnp.sum(before * onehot, axis=1)
    slot = route * cap + rank
    return slot[:, None] == jnp.arange(experts * cap, dtype=jnp.int32)[None, :]


def scaled_rows(rows, exponent):
    count, width = rows.shape
    blocks = exponent.shape[1]
    factor = 1.0 / jnp.left_shift(jnp.ones_like(exponent), exponent).astype(jnp.float32)
    scaled = rows.astype(jnp.float32).reshape(count, blocks, width // blocks) * factor[:, :, None]
    return scaled.reshape(count, width).astype(jnp.bfloat16)


def local(grad_rows, grad_exponent, gate, routing, saved_hidden, down_weight):
    experts = lax.axis_size("expert")
    slots = saved_hidden.shape[2]
    cap = slots // experts
    width = grad_rows.shape[1]
    dy_local = scaled_rows(grad_rows, grad_exponent)
    place = slot_table(routing[:, 0], experts, cap)
    place_low = place.astype(jnp.bfloat16)
    sent = lax.dot_general(
        place_low, dy_local, (((0,), (0,)), ((), ())), preferred_element_type=jnp.float32
    )
    sent = sent.astype(jnp.bfloat16).reshape(experts, cap, width)
    gate_sent = jnp.dot(gate, place_low, preferred_element_type=jnp.float32)
    gate_sent = gate_sent.astype(jnp.bfloat16).reshape(experts, cap)
    arrived, arrived_gate = (
        lax.all_to_all(sent, "expert", split_axis=0, concat_axis=0, tiled=True),
        lax.all_to_all(gate_sent, "expert", split_axis=0, concat_axis=0, tiled=True),
    )
    rows = arrived.reshape(slots, width)
    gates = arrived_gate.reshape(slots).astype(jnp.float32)
    weight = down_weight[0]
    hidden = saved_hidden[0, 0]
    raw = lax.dot_general(
        rows, weight, (((1,), (1,)), ((), ())), preferred_element_type=jnp.float32
    )
    hidden_grad = (gates[:, None] * raw).astype(jnp.bfloat16)
    output = jnp.dot(hidden, weight, preferred_element_type=jnp.float32)
    slot_grad = jnp.sum(rows.astype(jnp.float32) * output, axis=1)
    back = lax.all_to_all(
        slot_grad.reshape(experts, cap), "expert", split_axis=0, concat_axis=0, tiled=True
    )
    gate_grad = jnp.dot(
        place.astype(jnp.float32), back.reshape(slots), precision=lax.Precision.HIGHEST
    )
    weighted = (gates[:, None] * rows.astype(jnp.float32)).astype(jnp.bfloat16)
    weight_grad = lax.psum_scatter(
        lax.dot_general(
            hidden, weighted, (((0,), (0,)), ((), ())), preferred_element_type=jnp.float32
        ).astype(jnp.bfloat16),
        "dp",
        scatter_dimension=0,
        tiled=True,
    ).astype(jnp.float32)
    return (hidden_grad[None, None], weight_grad[None], gate_grad)


def solution(mesh):
    in_specs = (
        P(("dp", "expert"), None),
        P(("dp", "expert"), None),
        P(("dp", "expert")),
        P(("dp", "expert"), None),
        P("dp", "expert", None, None),
        P("expert", None, None),
    )
    out_specs = (P("dp", "expert", None, None), P("expert", "dp", None), P(("dp", "expert")))
    return jax.shard_map(local, mesh=mesh, in_specs=in_specs, out_specs=out_specs, check_vma=False)
```

profile of v0, /device:TPU:0, one launch (start us, length us, event | category | flops | bytes accessed | tf_op | source)
XLA Modules:
  0.0 146.6 jit_solution(17200733536191758812)
XLA Ops:
  7.2 0.8 fusion.29
  8.0 0.2 reduce_window_sum.11
  8.1 0.8 select_reduce_fusion
  9.0 0.7 fusion.31
  9.6 0.9 fusion.24
  10.5 0.7 all_to_all.20
  11.2 6.3 %all-to-all-start = ((bf16[4,1,34]{2,1,0:T(2,128)(2,1)}), bf16[4,1,34]{2,1,0:T(2,128)(2,1)S(1)}, u32[]{:S(2)}, u32[]{:S(2)}) async-start(bf16[4,1,34]{2,1,0:T(2,128)(2,1)} %all_to_all.20), calls=%async_computation | async-start | bytes 4096 | tf_op jit(solution)/shard_map/all_to_all | solution.py:39
  17.5 0.7 convert_divide_fusion
  18.2 1.6 %copy.16 = bf16[128,3584]{0,1:T(8,128)(2,1)S(1)} copy(bf16[128,3584]{1,0:T(8,128)(2,1)} %param.6) | data formatting | bytes 1835008 | tf_op args[0]
  19.8 0.2 fusion.8
  20.0 0.8 convolution_convert_fusion.1
  20.8 1.3 reshape.47
  22.0 0.9 all-to-all-done
  23.0 4.2 %all-to-all-start.1 = ((bf16[4,34,3584]{2,1,0:T(8,128)(2,1)}), bf16[4,34,3584]{2,1,0:T(8,128)(2,1)S(1)}, u32[]{:S(2)}, u32[]{:S(2)}) async-start(bf16[4,34,3584]{2,1,0:T(8,128)(2,1)} %reshape.47), calls=%async_computation.1 | async-start | bytes 2293760 | tf_op jit(solution)/shard_map/all_to_all | solution.py:38
  27.2 27.3 %all-to-all-done.1 = bf16[4,34,3584]{2,1,0:T(8,128)(2,1)S(1)} async-done(((bf16[4,34,3584]{2,1,0:T(8,128)(2,1)}), bf16[4,34,3584]{2,1,0:T(8,128)(2,1)S(1)}, u32[]{:S(2)}, u32[]{:S(2)}) %all-to-all-start.1) | async-done | bytes 974880 | tf_op jit(solution)/shard_map/all_to_all | solution.py:38
  54.4 0.3 multiply_convert_fusion
  54.7 0.3 convert_element_type.72
  55.0 5.2 %fusion.4 = bf16[1024,3584]{0,1:T(8,128)(2,1)} fusion(bf16[136,3584]{1,0:T(8,128)(2,1)S(1)} %convert_element_type.72, bf16[1,1,136,1024]{3,2,1,0:T(8,128)(2,1)S(1)} %copy-done), kind=kOutput, calls=%fused_computation.5 | convolution fusion | flops 1001914368 | bytes 8593408 | tf_op jit(solution)/shard_map/dot_general | solution.py:59
  60.2 10.0 %copy.18 = bf16[1024,3584]{1,0:T(8,128)(2,1)} copy(bf16[1024,3584]{0,1:T(8,128)(2,1)} %fusion.4) | data formatting | bytes 14680064
  70.3 0.3 reshape.48
  70.6 4.4 %fusion.9 = f32[136]{0:T(256)S(1)} fusion(bf16[1,1024,3584]{2,1,0:T(8,128)(2,1)} %param.11, bf16[136,3584]{1,0:T(8,128)(2,1)S(1)} %reshape.48, bf16[1,1,136,1024]{3,2,1,0:T(8,128)(2,1)S(1)} %copy-done), kind=kOutput, calls=%fused_computation.11 | convolution fusion | flops 999706496 | bytes 8593952 | tf_op jit(solution)/shard_map/dot_general | solution.py:49
  75.0 0.7 all_to_all.18
  75.7 3.2 %all-to-all-start.2 = ((f32[4,1,34]{2,1,0:T(1,128)}), f32[4,1,34]{2,1,0:T(1,128)S(1)}, u32[]{:S(2)}, u32[]{:S(2)}) async-start(f32[4,1,34]{2,1,0:T(1,128)} %all_to_all.18), calls=%async_computation.2 | async-start | bytes 4096 | tf_op jit(solution)/shard_map/all_to_all | solution.py:51
  78.9 7.4 %fusion.18 = bf16[1,1,136,1024]{3,2,1,0:T(8,128)(2,1)} fusion(bf16[136,3584]{1,0:T(8,128)(2,1)S(1)} %reshape.48, bf16[1,1024,3584]{2,1,0:T(8,128)(2,1)} %param.11, f32[136]{0:T(256)S(1)} %reshape.50), kind=kOutput, calls=%fused_computation.14 | convolution fusion | flops 998522880 | bytes 8593952 | tf_op jit(solution)/shard_map/dot_general | solution.py:45
  86.3 0.5 broadcast.16
  86.8 0.7 reduce.7
  87.5 0.1 reshape.55
  87.6 0.8 convolution_bitcast_fusion
  88.4 48.0 %reduce-scatter.4.cloned.1.call-done = bf16[128,3584]{1,0:T(8,128)(2,1)} async-done(((bf16[1024,3584]{1,0:T(8,128)(2,1)}), bf16[128,3584]{1,0:T(8,128)(2,1)}) %reduce-scatter.4.cloned.1.call-update) | async-done | bytes 917520
  136.4 1.5 %copy.19 = bf16[128,3584]{0,1:T(8,128)(2,1)S(1)} copy(bf16[128,3584]{1,0:T(8,128)(2,1)} %reduce-scatter.4.cloned.1.call-done) | data formatting | bytes 1835008
  138.0 0.1 bitcast_convert_fusion
  138.1 1.7 %copy.17 = f32[1,128,3584]{2,1,0:T(8,128)} copy(f32[1,128,3584]{1,2,0:T(8,128)S(1)} %bitcast_convert_fusion) | data formatting | bytes 3670016
  (9 shorter events, 0.1 us)
Async XLA Ops:
  7.2 47.8 %copy-start = (bf16[1,1,136,1024]{3,2,1,0:T(8,128)(2,1)S(1)}, bf16[1,1,136,1024]{3,2,1,0:T(8,128)(2,1)}, u32[]{:S(2)}) copy-start(bf16[1,1,136,1024]{3,2,1,0:T(8,128)(2,1)} %param.10) | copy-start | bytes 835588
  11.2 11.8 %all-to-all-start = ((bf16[4,1,34]{2,1,0:T(2,128)(2,1)}), bf16[4,1,34]{2,1,0:T(2,128)(2,1)S(1)}, u32[]{:S(2)}, u32[]{:S(2)}) async-start(bf16[4,1,34]{2,1,0:T(2,128)(2,1)} %all_to_all.20), calls=%async_computation | async-start | bytes 4096 | tf_op jit(solution)/shard_map/all_to_all | solution.py:39
  23.0 31.5 %all-to-all-start.1 = ((bf16[4,34,3584]{2,1,0:T(8,128)(2,1)}), bf16[4,34,3584]{2,1,0:T(8,128)(2,1)S(1)}, u32[]{:S(2)}, u32[]{:S(2)}) async-start(bf16[4,34,3584]{2,1,0:T(8,128)(2,1)} %reshape.47), calls=%async_computation.1 | async-start | bytes 2293760 | tf_op jit(solution)/shard_map/all_to_all | solution.py:38
  27.1 109.3 %reduce-scatter.4.cloned.1.call-start = ((), (), s32[]{:S(2)}) async-start(), calls=%async_computation.4 | async-start | bytes 8257536
  75.7 10.7 %all-to-all-start.2 = ((f32[4,1,34]{2,1,0:T(1,128)}), f32[4,1,34]{2,1,0:T(1,128)S(1)}, u32[]{:S(2)}, u32[]{:S(2)}) async-start(f32[4,1,34]{2,1,0:T(1,128)} %all_to_all.18), calls=%async_computation.2 | async-start | bytes 4096 | tf_op jit(solution)/shard_map/all_to_all | solution.py:51
Sparse Core Ops, SparseCore 0:
  70.3 66.0 reduce-scatter.3
where the time goes:
time: 147 us
  waiting for transfers between devices  76.2 us (52%)
  matrix products  19.4 us (13%)
  local copies, waits for them, and re-layouts  18.7 us (13%)
  between operations  14.1 us (10%)
  starting transfers between devices  13.7 us (9%)
  other arithmetic  4.42 us (3%)
    unnamed x2, waiting for transfers between devices  48.1 us
    all_to_all x1, waiting for transfers between devices, local(): lax.all_to_all(sent, 'expert', split_axis=0, concat_axis=0, tiled=True)  27.3 us
    unnamed x6, local copies, waits for them, and re-layouts  14.8 us
    dot_general x1, matrix products, local(): lax.dot_general(rows, weight, (((1,), (1,)), ((), ())), preferred_element...  7.44 us
    all_to_all x1, starting transfers between devices, local(): lax.all_to_all(gate_sent, 'expert', split_axis=0, concat_axis=0, tiled=True)  6.32 us
    dot_general x1, matrix products, local(): lax.dot_general(hidden, weighted, (((0,), (0,)), ((), ())), preferred_ele...  5.19 us
    dot_general x1, matrix products, local(): output = jnp.dot(hidden, weight, preferred_element_type=jnp.float32)  4.38 us
    all_to_all x1, starting transfers between devices, local(): lax.all_to_all(sent, 'expert', split_axis=0, concat_axis=0, tiled=True)  4.18 us
  transfers between devices with their start and end apart: 4, of which 3 were waited for; matrix products, arithmetic and copies ran while one was open for 13% of the time, Pallas kernels for 0%

commit v1 on v0

--- a/solution.py
+++ b/solution.py
@@ -1,7 +1,18 @@
+import functools
+
 import jax
 import jax.numpy as jnp
 from jax import lax
+from jax.experimental import pallas as pl
+from jax.experimental.pallas import tpu as pltpu
 from jax.sharding import PartitionSpec as P
+
+MESH = pl.DeviceIdType.MESH
+LANES = 128
+MAIN = 32
+EXTRA = 2
+BF = jnp.bfloat16
+F32 = jnp.float32
 
 
 def slot_table(route, experts, cap):
@@ -20,7 +31,7 @@
     return scaled.reshape(count, width).astype(jnp.bfloat16)
 
 
-def local(grad_rows, grad_exponent, gate, routing, saved_hidden, down_weight):
+def local_general(grad_rows, grad_exponent, gate, routing, saved_hidden, down_weight):
     experts = lax.axis_size("expert")
     slots = saved_hidden.shape[2]
     cap = slots // experts
@@ -46,8 +57,7 @@
         rows, weight, (((1,), (1,)), ((), ())), preferred_element_type=jnp.float32
     )
     hidden_grad = (gates[:, None] * raw).astype(jnp.bfloat16)
-    output = jnp.dot(hidden, weight, preferred_element_type=jnp.float32)
-    slot_grad = jnp.sum(rows.astype(jnp.float32) * output, axis=1)
+    slot_grad = jnp.sum(hidden.astype(jnp.float32) * raw, axis=1)
     back = lax.all_to_all(
         slot_grad.reshape(experts, cap), "expert", split_axis=0, concat_axis=0, tiled=True
     )
@@ -66,6 +76,373 @@
     return (hidden_grad[None, None], weight_grad[None], gate_grad)
 
 
+def iota(shape, axis):
+    return lax.broadcasted_iota(jnp.int32, shape, axis)
+
+
+def dot(a, b, dims=((1,), (0,)), precision=None):
+    return lax.dot_general(a, b, (dims, ((), ())), preferred_element_type=F32, precision=precision)
+
+
+def slot_of(i):
+    main = i < 4 * MAIN
+    j = i - 4 * MAIN
+    source = jnp.where(main, i >> 5, j >> 1)
+    rank = jnp.where(main, i & 31, MAIN + (j & 1))
+    return source, rank
+
+
+def pack_match(a, b):
+    q = a & 15
+    r = (q >= 7).astype(jnp.int32)
+    return (q < 14) & (b == (q - 7 * r) * 16 + (a >> 4) * 2 + r)
+
+
+def kernel(
+    cap,
+    chunks,
+    rows_ref,
+    exp_ref,
+    gate_ref,
+    route_ref,
+    hidden_ref,
+    weight_ref,
+    hidden_grad_ref,
+    weight_grad_ref,
+    gate_grad_ref,
+    dy,
+    sent,
+    sent_pack,
+    rows,
+    pack,
+    gath,
+    hblk,
+    hg,
+    wbuf,
+    rs_send,
+    rs_recv,
+    wg,
+    back_send,
+    back_recv,
+    pack_s,
+    pack_r,
+    z_s,
+    z_r,
+    h_s,
+    h_r,
+    core_s,
+    core_r,
+    nb_s,
+    nb_r,
+    relay_s,
+    relay_r,
+    rs_s,
+    rs_r,
+    back_s,
+    back_r,
+    w_sem,
+    out_sem,
+):
+    d = lax.axis_index("dp")
+    me = lax.axis_index("expert")
+    c = lax.rem(d, 2)
+    x = lax.rem(lax.div(d, 2), 2)
+    y = lax.div(d, 4)
+
+    def dp_at(yy, xx, cc):
+        return (yy * 2 + xx) * 2 + cc
+
+    width = rows_ref.shape[1]
+    wide = width // chunks
+    blocks = wide // LANES
+    total = 4 * MAIN + 16
+    other = dp_at(y, x, 1 - c)
+    near = (dp_at(y, 1 - x, c), dp_at(1 - y, x, c))
+    near_other = (dp_at(y, 1 - x, 1 - c), dp_at(1 - y, x, 1 - c))
+    peers_z = [lax.rem(me + o, 4) for o in (1, 2, 3)]
+
+    load = pltpu.make_async_copy(weight_ref, wbuf, w_sem)
+    load.start()
+
+    barrier = pltpu.get_barrier_semaphore()
+    for e in peers_z:
+        pl.semaphore_signal(barrier, inc=1, device_id=(d, e), device_id_type=MESH)
+    for p in (other,) + near + near_other:
+        pl.semaphore_signal(barrier, inc=1, device_id=(p, me), device_id_type=MESH)
+
+    def remote(src, dst, s, r, p, e):
+        return pltpu.make_async_remote_copy(
+            src_ref=src, dst_ref=dst, send_sem=s, recv_sem=r, device_id=(p, e), device_id_type=MESH
+        )
+
+    route = route_ref[...]
+    onehot = iota((16, LANES), 0) == route
+    onehot_low = onehot.astype(F32).astype(BF)
+    earlier = (iota((LANES, LANES), 0) < iota((LANES, LANES), 1)).astype(F32).astype(BF)
+    before = dot(onehot_low, earlier)
+    rank = jnp.sum(jnp.where(onehot, before, 0.0), axis=0, keepdims=True).astype(jnp.int32)
+    main_at = jnp.where(rank < MAIN, route * MAIN + rank, -1)
+    extra_at = jnp.where(rank < MAIN, -1, route * EXTRA + rank - MAIN)
+    place = (iota((LANES, LANES), 0) == main_at).astype(F32).astype(BF)
+    place_extra = (iota((16, LANES), 0) == extra_at).astype(F32).astype(BF)
+    rank_is = (iota((LANES, LANES), 0) == rank).astype(F32)
+    gate_slots = dot(
+        jnp.where(onehot, gate_ref[...], 0.0).astype(BF), rank_is.astype(BF), ((1,), (1,))
+    ).astype(BF)
+
+    factor = 1.0 / lax.shift_left(jnp.ones(exp_ref.shape, jnp.int32), exp_ref[...]).astype(F32)
+    for b in range(width // LANES):
+        columns = pl.ds(b * LANES, LANES)
+        dy[:, columns] = (rows_ref[:, columns].astype(F32) * factor[:, b : b + 1]).astype(BF)
+    packing = pack_match(iota((64, 16 * blocks), 0), iota((64, 16 * blocks), 1))
+    packing = packing.astype(F32).astype(BF)
+    at = iota((64, 16), 0)
+    gate_row = (((at & 15) == 14) & ((at >> 4) == iota((64, 16), 1))).astype(F32).astype(BF)
+    for k in range(chunks):
+        extra = dot(place_extra, dy[:, k * wide : (k + 1) * wide]).astype(BF)
+        stacked = jnp.concatenate(
+            [extra[:, b * LANES : (b + 1) * LANES] for b in range(blocks)], axis=0
+        )
+        tile = dot(packing, stacked)
+        if k == 0:
+            tile = tile + dot(gate_row, gate_slots)
+        sent_pack[:, k * 16 : (k + 1) * 16, :] = tile.astype(BF).reshape(4, 16, LANES)
+    pl.semaphore_wait(barrier, 8)
+    sends = []
+    pack_copies = []
+    for i, e in enumerate(peers_z):
+        copy = remote(sent_pack.at[e], pack.at[me], pack_s.at[i], pack_r.at[i], d, e)
+        copy.start()
+        pack_copies.append(copy)
+    pack[me] = sent_pack[me]
+    z_copies = []
+    own_rows = pl.ds(pl.multiple_of(me * MAIN, MAIN), MAIN)
+    for k in range(chunks):
+        sent[k] = dot(place, dy[:, k * wide : (k + 1) * wide]).astype(BF)
+        group = []
+        for i, e in enumerate(peers_z):
+            copy = remote(
+                sent.at[k, pl.ds(pl.multiple_of(e * MAIN, MAIN), MAIN)],
+                rows.at[k, own_rows],
+                z_s.at[k, i],
+                z_r.at[k, i],
+                d,
+                e,
+            )
+            copy.start()
+            group.append(copy)
+        rows[k, own_rows, :] = sent[k, own_rows, :]
+        z_copies.append(group)
+
+    slots = hidden_ref.shape[0]
+    source, in_source = slot_of(iota((total, slots), 0))
+    order = ((source < 4) & (iota((total, slots), 1) == source * cap + in_source))
+    hidden = dot(order.astype(F32).astype(BF), hidden_ref[...]).astype(BF)
+    for b in range(8):
+        hblk[b] = hidden[:, b * LANES : (b + 1) * LANES]
+    h_copies = []
+    for t in range(2):
+        for j, p in ((1, other), (2, near[t]), (3, near_other[t])):
+            pc = lax.rem(p, 2)
+            px = lax.rem(lax.div(p, 2), 2)
+            py = lax.div(p, 4)
+            partner = dp_at(1 - py, px, pc) if t == 0 else dp_at(py, 1 - px, pc)
+            for b, block in enumerate((partner, p)):
+                copy = remote(
+                    hblk.at[block], hg.at[t, b, j], h_s.at[t, b, j], h_r.at[t, b, j], p, me
+                )
+                copy.start()
+                h_copies.append(copy)
+        for b, block in enumerate((near[1 - t], d)):
+            hg[t, b, 0] = hblk[block]
+
+    for copy in pack_copies:
+        copy.wait_recv()
+    wide_at = iota((total, 64), 0)
+    source, _ = slot_of(wide_at)
+    pick = ((source < 4) & (iota((total, 64), 1) == source * 16 + 14)).astype(F32).astype(BF)
+    spread = dot(pick, pack[:, 0:16, :].reshape(64, LANES))
+    source, in_source = slot_of(iota((total, LANES), 0))
+    lane_is = (source < 4) & (iota((total, LANES), 1) == in_source)
+    gates = jnp.sum(jnp.where(lane_is, spread, 0.0), axis=1, keepdims=True)
+    unpacking = pack_match(iota((16 * blocks, 64), 1), iota((16 * blocks, 64), 0))
+    unpacking = unpacking.astype(F32).astype(BF)
+
+    core_copies, nb_copies, relay_copies, rs_copies, outs = [], [], [], [], []
+    raw = None
+
+    def own_chunk(k):
+        t = k % 2
+        spread_rows = dot(unpacking, pack[:, k * 16 : (k + 1) * 16, :].reshape(64, LANES))
+        for b in range(blocks):
+            rows[k, 4 * MAIN :, b * LANES : (b + 1) * LANES] = spread_rows[
+                b * 16 : (b + 1) * 16
+            ].astype(BF)
+        for copy in z_copies[k]:
+            copy.wait_recv()
+        gath[k, 0] = (gates * rows[k].astype(F32)).astype(BF)
+        copy = remote(gath.at[k, 0], gath.at[k, 2], nb_s.at[k], nb_r.at[k], near[t], me)
+        copy.start()
+        nb_copies.append(copy)
+        copy = remote(gath.at[k, 0], gath.at[k, 1], core_s.at[k], core_r.at[k], other, me)
+        copy.start()
+        core_copies.append(copy)
+
+    def relay_chunk(k):
+        nb_copies[k].wait_recv()
+        copy = remote(gath.at[k, 2], gath.at[k, 3], relay_s.at[k], relay_r.at[k], other, me)
+        copy.start()
+        relay_copies.append(copy)
+
+    def partial_chunk(k):
+        t = k % 2
+        core_copies[k].wait_recv()
+        relay_copies[k].wait_recv()
+        gathered = gath[k].reshape(4 * total, wide)
+        rs_send[k] = dot(hg[t, 0].reshape(4 * total, LANES), gathered, ((0,), (0,))).astype(BF)
+        copy = remote(rs_send.at[k], rs_recv.at[k], rs_s.at[k], rs_r.at[k], near[1 - t], me)
+        copy.start()
+        rs_copies.append(copy)
+        wg[k] = dot(hg[t, 1].reshape(4 * total, LANES), gathered, ((0,), (0,)))
+
+    for step in range(chunks + 1):
+        if step < chunks:
+            own_chunk(step)
+        if step >= 1:
+            relay_chunk(step - 1)
+        if step < chunks:
+            if step == 0:
+                load.wait()
+            term = dot(rows[step], wbuf[:, step * wide : (step + 1) * wide], ((1,), (1,)))
+            raw = term if raw is None else raw + term
+        if step == 1:
+            for copy in h_copies:
+                copy.wait_recv()
+        if step == chunks - 1:
+            slot_grad = jnp.sum(hidden.astype(F32) * raw, axis=1, keepdims=True)
+            in_lane = jnp.where(lane_is, slot_grad, 0.0)
+            tail = in_lane[4 * MAIN :]
+            tail_at = iota(tail.shape, 0) >> 1
+            for s in range(4):
+                line = jnp.sum(in_lane[s * MAIN : (s + 1) * MAIN], axis=0, keepdims=True)
+                line = line + jnp.sum(jnp.where(tail_at == s, tail, 0.0), axis=0, keepdims=True)
+                back_send[s] = jnp.broadcast_to(line, (8, LANES))
+            back_copies = []
+            for i, e in enumerate(peers_z):
+                copy = remote(back_send.at[e], back_recv.at[me], back_s.at[i], back_r.at[i], d, e)
+                copy.start()
+                back_copies.append(copy)
+            back_recv[me] = back_send[me]
+        if step >= 1:
+            partial_chunk(step - 1)
+
+    scaled = (gates * raw).astype(BF)
+    source, in_source = slot_of(iota((slots, total), 1))
+    order = ((source < 4) & (iota((slots, total), 0) == source * cap + in_source))
+    hidden_grad_ref[...] = dot(order.astype(F32).astype(BF), scaled).astype(BF)
+
+    for copy in back_copies:
+        copy.wait_recv()
+    taken = dot(
+        back_recv[...].reshape(4 * 8, LANES), rank_is, precision=lax.Precision.HIGHEST
+    )
+    answer = jnp.zeros((1, LANES), F32)
+    for e in range(4):
+        answer = answer + jnp.where(route == e, taken[e * 8 : e * 8 + 1], 0.0)
+    gate_grad_ref[...] = answer
+
+    for k in range(chunks):
+        rs_copies[k].wait_recv()
+        wg[k] = wg[k] + rs_recv[k].astype(F32)
+        copy = pltpu.make_async_copy(
+            wg.at[k], weight_grad_ref.at[:, pl.ds(k * wide, wide)], out_sem.at[k]
+        )
+        copy.start()
+        outs.append(copy)
+    for copy in (
+        pack_copies
+        + [one for group in z_copies for one in group]
+        + h_copies
+        + core_copies
+        + nb_copies
+        + relay_copies
+        + rs_copies
+        + back_copies
+    ):
+        copy.wait_send()
+    for copy in outs:
+        copy.wait()
+
+
+def local_fused(chunks, grad_rows, grad_exponent, gate, routing, saved_hidden, down_weight):
+    tokens, width = grad_rows.shape
+    slots, units = saved_hidden.shape[2:]
+    cap = slots // 4
+    wide = width // chunks
+    total = 4 * MAIN + 16
+    dma = pltpu.SemaphoreType.DMA
+    vmem = pl.BlockSpec(memory_space=pltpu.VMEM)
+    anywhere = pl.BlockSpec(memory_space=pl.ANY)
+    hidden_grad, weight_grad, gate_grad = pl.pallas_call(
+        functools.partial(kernel, cap, chunks),
+        out_shape=(
+            jax.ShapeDtypeStruct((slots, units), BF),
+            jax.ShapeDtypeStruct((units // 8, width), F32),
+            jax.ShapeDtypeStruct((1, tokens), F32),
+        ),
+        in_specs=[vmem] * 5 + [anywhere],
+        out_specs=(vmem, anywhere, vmem),
+        scratch_shapes=[
+            pltpu.VMEM((tokens, width), BF),
+            pltpu.VMEM((chunks, 4 * MAIN, wide), BF),
+            pltpu.VMEM((4, 16 * chunks, LANES), BF),
+            pltpu.VMEM((chunks, total, wide), BF),
+            pltpu.VMEM((4, 16 * chunks, LANES), BF),
+            pltpu.VMEM((chunks, 4, total, wide), BF),
+            pltpu.VMEM((8, total, LANES), BF),
+            pltpu.VMEM((2, 2, 4, total, LANES), BF),
+            pltpu.VMEM((units, width), BF),
+            pltpu.VMEM((chunks, LANES, wide), BF),
+            pltpu.VMEM((chunks, LANES, wide), BF),
+            pltpu.VMEM((chunks, LANES, wide), F32),
+            pltpu.VMEM((4, 8, LANES), F32),
+            pltpu.VMEM((4, 8, LANES), F32),
+            dma((3,)),
+            dma((3,)),
+            dma((chunks, 3)),
+            dma((chunks, 3)),
+            dma((2, 2, 4)),
+            dma((2, 2, 4)),
+            dma((chunks,)),
+            dma((chunks,)),
+            dma((chunks,)),
+            dma((chunks,)),
+            dma((chunks,)),
+            dma((chunks,)),
+            dma((chunks,)),
+            dma((chunks,)),
+            dma((3,)),
+            dma((3,)),
+            dma,
+            dma((chunks,)),
+        ],
+        compiler_params=pltpu.CompilerParams(
+            collective_id=0, has_side_effects=True, vmem_limit_bytes=56 * 1024 * 1024
+        ),
+        cost_estimate=pl.CostEstimate(
+            flops=4 * slots * units * width, bytes_accessed=2 * units * width, transcendentals=0
+        ),
+    )(
+        grad_rows,
+        grad_exponent,
+        gate.astype(F32).reshape(1, tokens),
+        routing.reshape(1, tokens),
+        saved_hidden.reshape(slots, units),
+        down_weight.reshape(units, width),
+    )
+    return (hidden_grad[None, None], weight_grad[None], gate_grad.reshape(tokens))
+
+
 def solution(mesh):
     in_specs = (
         P(("dp", "expert"), None),
@@ -76,4 +453,15 @@
         P("expert", None, None),
     )
     out_specs = (P("dp", "expert", None, None), P("expert", "dp", None), P(("dp", "expert")))
+
+    def local(grad_rows, grad_exponent, gate, routing, saved_hidden, down_weight):
+        args = (grad_rows, grad_exponent, gate, routing, saved_hidden, down_weight)
+        tokens, width = grad_rows.shape
+        slots, units = saved_hidden.shape[2:]
+        fits = mesh.shape["dp"] == 8 and mesh.shape["expert"] == 4 and tokens == LANES
+        fits = fits and slots == 4 * (MAIN + EXTRA) and units == 8 * LANES
+        if fits and width == 4 * 7 * LANES:
+            return local_fused(4, *args)
+        return local_general(*args)
+
     return jax.shard_map(local, mesh=mesh, in_specs=in_specs, out_specs=out_specs, check_vma=False)

time: 147 us -> 58.9 us (0.40)
  waiting for transfers between devices: 76.2 us -> 0 us
  Pallas kernels: 0 us -> 50.2 us
  matrix products: 19.4 us -> 0 us
  starting transfers between devices: 13.7 us -> 0 us
  between operations: 14.1 us -> 0.64 us
  local copies, waits for them, and re-layouts: 18.7 us -> 6.5 us
  other arithmetic: 4.42 us -> 1.17 us
    pallas_call x0 -> x1, Pallas kernels: none -> 50.2 us  [local_fused(): pl.pallas_call(functools.partial(kernel, cap, chunks), out_shape=(jax.Sha...]
    unnamed x2 -> x0, waiting for transfers between devices: 48.1 us -> none
    all_to_all x3 -> x0, waiting for transfers between devices: 28.2 us -> none  [the longest x1 27.3 us: local(): lax.all_to_all(sent, 'expert', split_axis=0, concat_axis=0, tiled=True)]
    dot_general x6 -> x0, matrix products: 19.4 us -> none  [the longest x1 7.44 us: local(): lax.dot_general(rows, weight, (((1,), (1,)), ((), ())), preferred_element...]
    all_to_all x3 -> x0, starting transfers between devices: 13.7 us -> none  [the longest x1 6.32 us: local(): lax.all_to_all(gate_sent, 'expert', split_axis=0, concat_axis=0, tiled=True)]
    unnamed x6, local copies, waits for them, and re-layouts: 14.8 us -> 6.5 us
    all_to_all x3 -> x0, local copies, waits for them, and re-layouts: 1.85 us -> none  [the longest x2 1.18 us: local(): lax.all_to_all(slot_grad.reshape(experts, cap), 'expert', split_axis=0, c...]
    reshape x3 -> x0, local copies, waits for them, and re-layouts: 1.65 us -> none  [the longest x1 1.28 us: local(): sent = sent.astype(jnp.bfloat16).reshape(experts, cap, width)]
  transfers between devices with their start and end apart: 4 -> 0, of which waited for: 3 -> 0; matrix products, arithmetic and copies ran while one was open for 13% -> 0% of each run, Pallas kernels for 0% -> 0%
where the time goes in v1:
time: 58.9 us; the launch traced here: 58.5 us
  Pallas kernels  50.2 us (85%)
  local copies, waits for them, and re-layouts  6.5 us (11%)
  other arithmetic  1.17 us (2%)
  between operations  0.64 us (1%)
    pallas_call x1, Pallas kernels, local_fused(): pl.pallas_call(functools.partial(kernel, cap, chunks), out_shape=(jax.Sha...  50.2 us
    unnamed x6, local copies, waits for them, and re-layouts  6.5 us

profile of v1, /device:TPU:0, one launch (start us, length us, event | category | flops | bytes accessed | tf_op | source)
XLA Modules:
  0.0 58.5 jit_solution(8461638118382650495)
XLA Ops:
  0.6 1.2 %bitcast_convert_fusion.gate_ref = f32[1,128]{1,0:T(1,128)} fusion(bf16[128]{0:T(256)(128)(2,1)} %param.8), kind=kLoop, calls=%fused_computation | loop fusion | flops 128 | bytes 768 | tf_op jit(solution)/shard_map/reshape | solution.py:438
  1.8 1.4 %copy.9.exp_ref = s32[128,28]{1,0:T(8,128)} copy(s32[128,28]{0,1:T(8,128)} %param.7) | data formatting | bytes 28672 | tf_op args[1]
  3.2 50.2 %shard_map.85 = (bf16[136,1024]{1,0:T(8,128)(2,1)}, f32[128,3584]{1,0:T(8,128)}, f32[1,128]{1,0:T(1,128)}) custom-call(bf16[128,3584]{1,0:T(8,128)(2,1)} %rows_ref.1, s32[128,28]{1,0:T(8,128)} %copy.9.exp_ref, f32[1,128]{1,0:T(1,128)} %bitcast_convert_fusion.gate_ref, s32[1,128]{1,0:T(1,128)} %bitcast.13, bf16[136,1024]{1,0:T(8,128)(2,1)} %bitcast.11, ...), custom_call_target="tpu_custom_call" | custom-call | flops 1996488704 | bytes 7340032 | tf_op jit(solution)/shard_map/pallas_call | solution.py:386
  53.4 1.7 %copy.13 = bf16[1,1,136,1024]{3,2,1,0:T(8,128)(2,1)} copy(bf16[1,1,136,1024]{3,2,1,0:T(8,128)(2,1)} %bitcast.12) | data formatting | bytes 557056
  55.1 0.0 copy-start
  55.1 2.9 %copy.14 = f32[1,128,3584]{2,1,0:T(8,128)} copy(f32[1,128,3584]{2,1,0:T(8,128)} %bitcast.10) | data formatting | bytes 3670016
  58.0 0.0 copy-done
  58.0 0.5 copy.15
Async XLA Ops:
  55.1 2.9 %copy-start = (f32[1,128]{1,0:T(1,128)S(1)}, f32[1,128]{1,0:T(1,128)}, u32[]{:S(2)}) copy-start(f32[1,128]{1,0:T(1,128)} %get-tuple-element.8) | copy-start | bytes 1540

commit v2 on v1

--- a/solution.py
+++ b/solution.py
@@ -11,6 +11,7 @@
 LANES = 128
 MAIN = 32
 EXTRA = 2
+GATE_ROW = 56
 BF = jnp.bfloat16
 F32 = jnp.float32
 
@@ -92,15 +93,16 @@
     return source, rank
 
 
-def pack_match(a, b):
-    q = a & 15
-    r = (q >= 7).astype(jnp.int32)
-    return (q < 14) & (b == (q - 7 * r) * 16 + (a >> 4) * 2 + r)
+def pack_match(blocks, a, b):
+    q = a & 63
+    r = (q >= blocks).astype(jnp.int32)
+    return (q < 2 * blocks) & (b == (q - blocks * r) * 16 + (a >> 6) * 2 + r)
 
 
 def kernel(
     cap,
     chunks,
+    ahead,
     rows_ref,
     exp_ref,
     gate_ref,
@@ -141,7 +143,6 @@
     back_s,
     back_r,
     w_sem,
-    out_sem,
 ):
     d = lax.axis_index("dp")
     me = lax.axis_index("expert")
@@ -155,6 +156,8 @@
     width = rows_ref.shape[1]
     wide = width // chunks
     blocks = wide // LANES
+    half = wide // 2
+    all_blocks = width // LANES
     total = 4 * MAIN + 16
     other = dp_at(y, x, 1 - c)
     near = (dp_at(y, 1 - x, c), dp_at(1 - y, x, c))
@@ -191,34 +194,32 @@
     ).astype(BF)
 
     factor = 1.0 / lax.shift_left(jnp.ones(exp_ref.shape, jnp.int32), exp_ref[...]).astype(F32)
-    for b in range(width // LANES):
+    factor = jnp.concatenate([factor, jnp.zeros((32 - all_blocks, LANES), F32)], axis=0).T
+    for b in range(all_blocks):
         columns = pl.ds(b * LANES, LANES)
         dy[:, columns] = (rows_ref[:, columns].astype(F32) * factor[:, b : b + 1]).astype(BF)
-    packing = pack_match(iota((64, 16 * blocks), 0), iota((64, 16 * blocks), 1))
-    packing = packing.astype(F32).astype(BF)
-    at = iota((64, 16), 0)
-    gate_row = (((at & 15) == 14) & ((at >> 4) == iota((64, 16), 1))).astype(F32).astype(BF)
-    for k in range(chunks):
-        extra = dot(place_extra, dy[:, k * wide : (k + 1) * wide]).astype(BF)
-        stacked = jnp.concatenate(
-            [extra[:, b * LANES : (b + 1) * LANES] for b in range(blocks)], axis=0
-        )
-        tile = dot(packing, stacked)
+    extra = dot(place_extra, dy[...]).astype(BF)
+    stacked = jnp.concatenate(
+        [extra[:, b * LANES : (b + 1) * LANES] for b in range(all_blocks)], axis=0
+    )
+    at = (4 * 64, 16 * all_blocks)
+    packing = pack_match(all_blocks, iota(at, 0), iota(at, 1)).astype(F32).astype(BF)
+    at = iota((4 * 64, 16), 0)
+    gate_row = (((at & 63) == GATE_ROW) & ((at >> 6) == iota((4 * 64, 16), 1))).astype(F32)
+    tile = dot(packing, stacked) + dot(gate_row.astype(BF), gate_slots)
+    sent_pack[...] = tile.astype(BF).reshape(4, 64, LANES)
+    own_rows = pl.ds(pl.multiple_of(me * MAIN, MAIN), MAIN)
+    z_copies = []
+
+    def dispatch(k):
+        sent[k] = dot(place, dy[:, k * wide : (k + 1) * wide]).astype(BF)
         if k == 0:
-            tile = tile + dot(gate_row, gate_slots)
-        sent_pack[:, k * 16 : (k + 1) * 16, :] = tile.astype(BF).reshape(4, 16, LANES)
-    pl.semaphore_wait(barrier, 8)
-    sends = []
-    pack_copies = []
-    for i, e in enumerate(peers_z):
-        copy = remote(sent_pack.at[e], pack.at[me], pack_s.at[i], pack_r.at[i], d, e)
-        copy.start()
-        pack_copies.append(copy)
-    pack[me] = sent_pack[me]
-    z_copies = []
-    own_rows = pl.ds(pl.multiple_of(me * MAIN, MAIN), MAIN)
-    for k in range(chunks):
-        sent[k] = dot(place, dy[:, k * wide : (k + 1) * wide]).astype(BF)
+            pl.semaphore_wait(barrier, 8)
+            for i, e in enumerate(peers_z):
+                copy = remote(sent_pack.at[e], pack.at[me], pack_s.at[i], pack_r.at[i], d, e)
+                copy.start()
+                pack_copies.append(copy)
+            pack[me] = sent_pack[me]
         group = []
         for i, e in enumerate(peers_z):
             copy = remote(
@@ -233,6 +234,10 @@
             group.append(copy)
         rows[k, own_rows, :] = sent[k, own_rows, :]
         z_copies.append(group)
+
+    pack_copies = []
+    for k in range(ahead):
+        dispatch(k)
 
     slots = hidden_ref.shape[0]
     source, in_source = slot_of(iota((total, slots), 0))
@@ -258,52 +263,69 @@
 
     for copy in pack_copies:
         copy.wait_recv()
-    wide_at = iota((total, 64), 0)
-    source, _ = slot_of(wide_at)
-    pick = ((source < 4) & (iota((total, 64), 1) == source * 16 + 14)).astype(F32).astype(BF)
-    spread = dot(pick, pack[:, 0:16, :].reshape(64, LANES))
+    at = (total, 4 * 64)
+    source, _ = slot_of(iota(at, 0))
+    pick = ((source < 4) & (iota(at, 1) == source * 64 + GATE_ROW)).astype(F32).astype(BF)
+    spread = dot(pick, pack[...].reshape(4 * 64, LANES))
     source, in_source = slot_of(iota((total, LANES), 0))
     lane_is = (source < 4) & (iota((total, LANES), 1) == in_source)
     gates = jnp.sum(jnp.where(lane_is, spread, 0.0), axis=1, keepdims=True)
-    unpacking = pack_match(iota((16 * blocks, 64), 1), iota((16 * blocks, 64), 0))
-    unpacking = unpacking.astype(F32).astype(BF)
-
-    core_copies, nb_copies, relay_copies, rs_copies, outs = [], [], [], [], []
+
+    core_copies, nb_copies, relay_copies, rs_copies = [], [], [], []
     raw = None
 
     def own_chunk(k):
-        t = k % 2
-        spread_rows = dot(unpacking, pack[:, k * 16 : (k + 1) * 16, :].reshape(64, LANES))
+        at = (16 * blocks, 4 * 64)
+        unpacking = pack_match(all_blocks, iota(at, 1), iota(at, 0) + k * 16 * blocks)
+        spread_rows = dot(unpacking.astype(F32).astype(BF), pack[...].reshape(4 * 64, LANES))
         for b in range(blocks):
             rows[k, 4 * MAIN :, b * LANES : (b + 1) * LANES] = spread_rows[
                 b * 16 : (b + 1) * 16
             ].astype(BF)
         for copy in z_copies[k]:
             copy.wait_recv()
-        gath[k, 0] = (gates * rows[k].astype(F32)).astype(BF)
-        copy = remote(gath.at[k, 0], gath.at[k, 2], nb_s.at[k], nb_r.at[k], near[t], me)
-        copy.start()
-        nb_copies.append(copy)
+        if k + ahead < chunks:
+            dispatch(k + ahead)
+        pair = []
+        for t in range(2):
+            part = rows[k, :, t * half : (t + 1) * half].astype(F32)
+            gath[k, 0, t] = (gates * part).astype(BF)
+            copy = remote(
+                gath.at[k, 0, t], gath.at[k, 2, t], nb_s.at[k, t], nb_r.at[k, t], near[t], me
+            )
+            copy.start()
+            pair.append(copy)
+        nb_copies.append(pair)
         copy = remote(gath.at[k, 0], gath.at[k, 1], core_s.at[k], core_r.at[k], other, me)
         copy.start()
         core_copies.append(copy)
 
     def relay_chunk(k):
-        nb_copies[k].wait_recv()
+        for copy in nb_copies[k]:
+            copy.wait_recv()
         copy = remote(gath.at[k, 2], gath.at[k, 3], relay_s.at[k], relay_r.at[k], other, me)
         copy.start()
         relay_copies.append(copy)
 
     def partial_chunk(k):
-        t = k % 2
         core_copies[k].wait_recv()
         relay_copies[k].wait_recv()
-        gathered = gath[k].reshape(4 * total, wide)
-        rs_send[k] = dot(hg[t, 0].reshape(4 * total, LANES), gathered, ((0,), (0,))).astype(BF)
-        copy = remote(rs_send.at[k], rs_recv.at[k], rs_s.at[k], rs_r.at[k], near[1 - t], me)
-        copy.start()
-        rs_copies.append(copy)
-        wg[k] = dot(hg[t, 1].reshape(4 * total, LANES), gathered, ((0,), (0,)))
+        pair = []
+        for t in range(2):
+            gathered = gath[k, :, t].reshape(4 * total, half)
+            away = dot(hg[t, 0].reshape(4 * total, LANES), gathered, ((0,), (0,)))
+            rs_send[k, t] = away.astype(BF)
+            copy = remote(
+                rs_send.at[k, t], rs_recv.at[k, t], rs_s.at[k, t], rs_r.at[k, t], near[1 - t], me
+            )
+            copy.start()
+            pair.append(copy)
+        rs_copies.append(pair)
+        for t in range(2):
+            gathered = gath[k, :, t].reshape(4 * total, half)
+            wg[k, :, t * half : (t + 1) * half] = dot(
+                hg[t, 1].reshape(4 * total, LANES), gathered, ((0,), (0,))
+            )
 
     for step in range(chunks + 1):
         if step < chunks:
@@ -352,29 +374,57 @@
     gate_grad_ref[...] = answer
 
     for k in range(chunks):
-        rs_copies[k].wait_recv()
-        wg[k] = wg[k] + rs_recv[k].astype(F32)
-        copy = pltpu.make_async_copy(
-            wg.at[k], weight_grad_ref.at[:, pl.ds(k * wide, wide)], out_sem.at[k]
-        )
-        copy.start()
-        outs.append(copy)
+        for t in range(2):
+            rs_copies[k][t].wait_recv()
+            columns = pl.ds(t * half, half)
+            target = pl.ds(k * wide + t * half, half)
+            weight_grad_ref[:, target] = wg[k, :, columns] + rs_recv[k, t].astype(F32)
     for copy in (
         pack_copies
         + [one for group in z_copies for one in group]
         + h_copies
         + core_copies
-        + nb_copies
+        + [one for pair in nb_copies for one in pair]
         + relay_copies
-        + rs_copies
+        + [one for pair in rs_copies for one in pair]
         + back_copies
     ):
         copy.wait_send()
-    for copy in outs:
+
+
+PIECES = 8
+
+
+def finish_kernel(*refs):
+    sources, targets, sem = refs[:3], refs[3:6], refs[6]
+    copies = []
+    step = sources[1].shape[0] // PIECES
+    for i in range(PIECES):
+        at = pl.ds(i * step, step)
+        copies.append(
+            pltpu.make_async_copy(sources[1].at[at], targets[1].at[at], sem.at[i])
+        )
+    for i, j in ((0, PIECES), (2, PIECES + 1)):
+        copies.append(pltpu.make_async_copy(sources[i], targets[i], sem.at[j]))
+    for copy in copies:
+        copy.start()
+    for copy in copies:
         copy.wait()
 
 
-def local_fused(chunks, grad_rows, grad_exponent, gate, routing, saved_hidden, down_weight):
+def finish(*arrays):
+    anywhere = pl.BlockSpec(memory_space=pl.ANY)
+    return pl.pallas_call(
+        finish_kernel,
+        out_shape=tuple(jax.ShapeDtypeStruct(a.shape, a.dtype) for a in arrays),
+        in_specs=[pl.BlockSpec(memory_space=pltpu.VMEM)] * 3,
+        out_specs=(anywhere,) * 3,
+        scratch_shapes=[pltpu.SemaphoreType.DMA((PIECES + 2,))],
+        compiler_params=pltpu.CompilerParams(vmem_limit_bytes=16 * 1024 * 1024),
+    )(*arrays)
+
+
+def local_fused(chunks, ahead, grad_rows, grad_exponent, gate, routing, saved_hidden, down_weight):
     tokens, width = grad_rows.shape
     slots, units = saved_hidden.shape[2:]
     cap = slots // 4
@@ -384,26 +434,26 @@
     vmem = pl.BlockSpec(memory_space=pltpu.VMEM)
     anywhere = pl.BlockSpec(memory_space=pl.ANY)
     hidden_grad, weight_grad, gate_grad = pl.pallas_call(
-        functools.partial(kernel, cap, chunks),
+        functools.partial(kernel, cap, chunks, ahead),
         out_shape=(
-            jax.ShapeDtypeStruct((slots, units), BF),
-            jax.ShapeDtypeStruct((units // 8, width), F32),
-            jax.ShapeDtypeStruct((1, tokens), F32),
+            pltpu.VMEM((slots, units), BF),
+            pltpu.VMEM((units // 8, width), F32),
+            pltpu.VMEM((1, tokens), F32),
         ),
         in_specs=[vmem] * 5 + [anywhere],
-        out_specs=(vmem, anywhere, vmem),
+        out_specs=(vmem, vmem, vmem),
         scratch_shapes=[
             pltpu.VMEM((tokens, width), BF),
             pltpu.VMEM((chunks, 4 * MAIN, wide), BF),
-            pltpu.VMEM((4, 16 * chunks, LANES), BF),
+            pltpu.VMEM((4, 64, LANES), BF),
             pltpu.VMEM((chunks, total, wide), BF),
-            pltpu.VMEM((4, 16 * chunks, LANES), BF),
-            pltpu.VMEM((chunks, 4, total, wide), BF),
+            pltpu.VMEM((4, 64, LANES), BF),
+            pltpu.VMEM((chunks, 4, 2, total, wide // 2), BF),
             pltpu.VMEM((8, total, LANES), BF),
             pltpu.VMEM((2, 2, 4, total, LANES), BF),
             pltpu.VMEM((units, width), BF),
-            pltpu.VMEM((chunks, LANES, wide), BF),
-            pltpu.VMEM((chunks, LANES, wide), BF),
+            pltpu.VMEM((chunks, 2, LANES, wide // 2), BF),
+            pltpu.VMEM((chunks, 2, LANES, wide // 2), BF),
             pltpu.VMEM((chunks, LANES, wide), F32),
             pltpu.VMEM((4, 8, LANES), F32),
             pltpu.VMEM((4, 8, LANES), F32),
@@ -415,31 +465,31 @@
             dma((2, 2, 4)),
             dma((chunks,)),
             dma((chunks,)),
+            dma((chunks, 2)),
+            dma((chunks, 2)),
             dma((chunks,)),
             dma((chunks,)),
-            dma((chunks,)),
-            dma((chunks,)),
-            dma((chunks,)),
-            dma((chunks,)),
+            dma((chunks, 2)),
+            dma((chunks, 2)),
             dma((3,)),
             dma((3,)),
             dma,
-            dma((chunks,)),
         ],
         compiler_params=pltpu.CompilerParams(
-            collective_id=0, has_side_effects=True, vmem_limit_bytes=56 * 1024 * 1024
+            collective_id=0, has_side_effects=True, vmem_limit_bytes=58 * 1024 * 1024
         ),
         cost_estimate=pl.CostEstimate(
             flops=4 * slots * units * width, bytes_accessed=2 * units * width, transcendentals=0
         ),
     )(
         grad_rows,
-        grad_exponent,
+        grad_exponent.T,
         gate.astype(F32).reshape(1, tokens),
         routing.reshape(1, tokens),
         saved_hidden.reshape(slots, units),
         down_weight.reshape(units, width),
     )
+    hidden_grad, weight_grad, gate_grad = finish(hidden_grad, weight_grad, gate_grad)
     return (hidden_grad[None, None], weight_grad[None], gate_grad.reshape(tokens))
 
 
@@ -461,7 +511,7 @@
         fits = mesh.shape["dp"] == 8 and mesh.shape["expert"] == 4 and tokens == LANES
         fits = fits and slots == 4 * (MAIN + EXTRA) and units == 8 * LANES
         if fits and width == 4 * 7 * LANES:
-            return local_fused(4, *args)
+            return local_fused(7, 2, *args)
         return local_general(*args)
 
     return jax.shard_map(local, mesh=mesh, in_specs=in_specs, out_specs=out_specs, check_vma=False)

time: 58.9 us -> 47.6 us (0.81)
  local copies, waits for them, and re-layouts: 6.5 us -> 0 us
  Pallas kernels: 50.2 us -> 45.7 us
    unnamed x6 -> x0, local copies, waits for them, and re-layouts: 6.5 us -> none
    pallas_call x1 -> x2, Pallas kernels: 50.2 us -> 45.7 us  [the longest x1 44.3 us: local_fused(): pl.pallas_call(functools.partial(kernel, cap, chunks, ahead), out_shape=(...]
where the time goes in v2:
time: 47.6 us; the launch traced here: 47.5 us
  Pallas kernels  45.7 us (96%)
  other arithmetic  1.17 us (2%)
  between operations  0.64 us (1%)
    pallas_call x1, Pallas kernels, local_fused(): pl.pallas_call(functools.partial(kernel, cap, chunks, ahead), out_shape=(...  44.3 us
    pallas_call x1, Pallas kernels, finish(): pl.pallas_call(finish_kernel, out_shape=tuple((jax.ShapeDtypeStruct(a.sha...  1.41 us
    reshape x1, other arithmetic, local_fused(): gate.astype(F32).reshape(1, tokens)  1.17 us

profile of v2, /device:TPU:0, one launch (start us, length us, event | category | flops | bytes accessed | tf_op | source)
XLA Modules:
  0.0 47.5 jit_solution(7996637988106086695)
XLA Ops:
  0.6 1.2 %bitcast_convert_fusion.gate_ref = f32[1,128]{1,0:T(1,128)} fusion(bf16[128]{0:T(256)(128)(2,1)} %param.8), kind=kLoop, calls=%fused_computation | loop fusion | flops 128 | bytes 768 | tf_op jit(solution)/shard_map/reshape | solution.py:487
  1.8 44.3 %shard_map.85 = (bf16[136,1024]{1,0:T(8,128)(2,1)S(1)}, f32[128,3584]{1,0:T(8,128)S(1)}, f32[1,128]{1,0:T(1,128)S(1)}) custom-call(bf16[128,3584]{1,0:T(8,128)(2,1)} %rows_ref.1, s32[28,128]{1,0:T(8,128)} %bitcast.12, f32[1,128]{1,0:T(1,128)} %bitcast_convert_fusion.gate_ref, s32[1,128]{1,0:T(1,128)} %bitcast.13, bf16[136,1024]{1,0:T(8,128)(2,1)} %bitcast.11, ...), custom_call_target="tpu_custom_call" | custom-call | flops 1996488704 | bytes 7340032 | tf_op jit(solution)/shard_map/pallas_call | solution.py:436
  46.1 1.4 %shard_map.86 = (bf16[136,1024]{1,0:T(8,128)(2,1)}, f32[128,3584]{1,0:T(8,128)}, f32[1,128]{1,0:T(1,128)}) custom-call(bf16[136,1024]{1,0:T(8,128)(2,1)S(1)} %get-tuple-element.9.refs_0_, f32[128,3584]{1,0:T(8,128)S(1)} %get-tuple-element.10.refs_1_, f32[1,128]{1,0:T(1,128)S(1)} %get-tuple-element.11.refs_2_), custom_call_target="tpu_custom_call" | custom-call | tf_op jit(solution)/shard_map/pallas_call | solution.py:417

commit v3 on v2

--- a/solution.py
+++ b/solution.py
@@ -190,7 +190,7 @@
     place_extra = (iota((16, LANES), 0) == extra_at).astype(F32).astype(BF)
     rank_is = (iota((LANES, LANES), 0) == rank).astype(F32)
     gate_slots = dot(
-        jnp.where(onehot, gate_ref[...], 0.0).astype(BF), rank_is.astype(BF), ((1,), (1,))
+        jnp.where(onehot, gate_ref[...].astype(F32).reshape(1, LANES), 0.0).astype(BF), rank_is.astype(BF), ((1,), (1,))
     ).astype(BF)
 
     factor = 1.0 / lax.shift_left(jnp.ones(exp_ref.shape, jnp.int32), exp_ref[...]).astype(F32)
@@ -327,10 +327,17 @@
                 hg[t, 1].reshape(4 * total, LANES), gathered, ((0,), (0,))
             )
 
-    for step in range(chunks + 1):
+    def add_chunk(k):
+        for t in range(2):
+            rs_copies[k][t].wait_recv()
+            columns = pl.ds(t * half, half)
+            target = pl.ds(k * wide + t * half, half)
+            weight_grad_ref[:, target] = wg[k, :, columns] + rs_recv[k, t].astype(F32)
+
+    for step in range(chunks + 2):
         if step < chunks:
             own_chunk(step)
-        if step >= 1:
+        if 1 <= step <= chunks:
             relay_chunk(step - 1)
         if step < chunks:
             if step == 0:
@@ -355,8 +362,10 @@
                 copy.start()
                 back_copies.append(copy)
             back_recv[me] = back_send[me]
-        if step >= 1:
-            partial_chunk(step - 1)
+        if step >= 2:
+            partial_chunk(step - 2)
+        if step >= 5:
+            add_chunk(step - 5)
 
     scaled = (gates * raw).astype(BF)
     source, in_source = slot_of(iota((slots, total), 1))
@@ -373,12 +382,8 @@
         answer = answer + jnp.where(route == e, taken[e * 8 : e * 8 + 1], 0.0)
     gate_grad_ref[...] = answer
 
-    for k in range(chunks):
-        for t in range(2):
-            rs_copies[k][t].wait_recv()
-            columns = pl.ds(t * half, half)
-            target = pl.ds(k * wide + t * half, half)
-            weight_grad_ref[:, target] = wg[k, :, columns] + rs_recv[k, t].astype(F32)
+    for k in range(chunks - 3, chunks):
+        add_chunk(k)
     for copy in (
         pack_copies
         + [one for group in z_copies for one in group]
@@ -484,7 +489,7 @@
     )(
         grad_rows,
         grad_exponent.T,
-        gate.astype(F32).reshape(1, tokens),
+        gate,
         routing.reshape(1, tokens),
         saved_hidden.reshape(slots, units),
         down_weight.reshape(units, width),

time: 47.6 us -> 44.9 us (0.943)
  Pallas kernels: 45.7 us -> 44.1 us
  other arithmetic: 1.17 us -> 0 us
    pallas_call x1, Pallas kernels: 44.3 us -> 42.7 us  [local_fused(): pl.pallas_call(functools.partial(kernel, cap, chunks, ahead), out_shape=(...]
    reshape x1 -> x0, other arithmetic: 1.17 us -> none  [local_fused(): gate.astype(F32).reshape(1, tokens)]
where the time goes in v3:
time: 44.9 us; the launch traced here: 44.8 us
  Pallas kernels  44.1 us (98%)
  between operations  0.64 us (1%)
    pallas_call x1, Pallas kernels, local_fused(): pl.pallas_call(functools.partial(kernel, cap, chunks, ahead), out_shape=(...  42.7 us
    pallas_call x1, Pallas kernels, finish(): pl.pallas_call(finish_kernel, out_shape=tuple((jax.ShapeDtypeStruct(a.sha...  1.41 us

profile of v3, /device:TPU:0, one launch (start us, length us, event | category | flops | bytes accessed | tf_op | source)
XLA Modules:
  0.0 44.8 jit_solution(4088693264430175753)
XLA Ops:
  0.6 42.7 %shard_map.85 = (bf16[136,1024]{1,0:T(8,128)(2,1)S(1)}, f32[128,3584]{1,0:T(8,128)S(1)}, f32[1,128]{1,0:T(1,128)S(1)}) custom-call(bf16[128,3584]{1,0:T(8,128)(2,1)} %rows_ref.1, s32[28,128]{1,0:T(8,128)} %bitcast.9, bf16[128]{0:T(256)(128)(2,1)} %gate_ref.1, s32[1,128]{1,0:T(1,128)} %bitcast.10, bf16[136,1024]{1,0:T(8,128)(2,1)} %bitcast.8, ...), custom_call_target="tpu_custom_call" | custom-call | flops 1996488704 | bytes 7340032 | tf_op jit(solution)/shard_map/pallas_call | solution.py:441
  43.4 1.4 %shard_map.86 = (bf16[136,1024]{1,0:T(8,128)(2,1)}, f32[128,3584]{1,0:T(8,128)}, f32[1,128]{1,0:T(1,128)}) custom-call(bf16[136,1024]{1,0:T(8,128)(2,1)S(1)} %get-tuple-element.9.refs_0_, f32[128,3584]{1,0:T(8,128)S(1)} %get-tuple-element.10.refs_1_, f32[1,128]{1,0:T(1,128)S(1)} %get-tuple-element.11.refs_2_), custom_call_target="tpu_custom_call" | custom-call | tf_op jit(solution)/shard_map/pallas_call | solution.py:422
